TPU v7x, 32 devices: a whole 2x2x4 slice. The times are simulated.
32 devices in a mesh: parts: 2 (over y), wide: 4 (over x, core), tensor: 4 (over z).
Axes of the slice: x: 2, y: 2, z: 4, core: 2. Of those that a mesh axis runs over, the one named last changes fastest.
Arguments:
- tokens: bfloat16 [2048, 8192], P(('parts', 'wide'), 'tensor'), parts along dimension 0, may hold values from -300 to 300
- attention_norm_gain: bfloat16 [8192], P('tensor'), may hold values from 0.099609375 to 1.8984375
- key_value_weight: bfloat16 [8192, 2048], P('tensor'), may hold values from -0.0625 to 0.0625
- adapter_down_weight: bfloat16 [64, 8192, 128], P(('parts', 'wide'), 'tensor'), parts along dimension 0, may hold values from -0.0625 to 0.0625
- adapter_up_weight: bfloat16 [64, 64, 2048], P(('parts', 'wide'), None, 'tensor'), parts along dimension 0, may hold values from -0.75 to 0.75
- request_adapter: int32 [2048], P(('parts', 'wide')), parts along dimension 0, may hold values from 0 to 31, as said below
- adapter_storage_row: int32 [64], P('parts'), parts along dimension 0, may hold values from 0 to 31, as said below
- cached_token_length: int32 [2048], P(('parts', 'wide')), parts along dimension 0, may hold values from 1 to 8192
Outputs:
- kv_entries: bfloat16 [2048, 2048], P(('parts', 'wide'), 'tensor'), parts along dimension 0
There are 2 independent parts, one for each index of `parts`. A program takes and returns all parts, laid end to end along the dimension named above; an argument that names none is the same for every part. Nothing has to cross between parts.
Inputs may be any that keep to these rules, and one draw needn't show every extreme that they name: A permutation; adapter a lies in storage row adapter_storage_row[a], held by wide index adapter_storage_row[a] // 8. `request_adapter`: among the 256 requests of one wide index, at most 104 have adapters held by any one wide index; one wide index holds the adapters of exactly 104 requests of every wide index.
All inputs are finite; a program needn't handle non-finite values.
Results may differ from a plain program's by a relative error of at most 0.0057.
Values may be sent and summed in bfloat16 or wider, within the bound.
No kernel may reach another device: no remote copies, remote signals or barrier semaphores. Data moves between devices by JAX's collectives and lax.ppermute only.
A program may use at most 64 MiB of HBM per device.

v0:
```python
import math

import jax
import jax.numpy as jnp
from jax import lax
from jax.sharding import PartitionSpec as P

MODEL_WIDTH = 8192
HEAD = 128


EPSILON = 1e-05
ROPE_BASE = 500000.0


def rotate_keys(joined_output, positions, column_start, head_size):
    row_count = joined_output.shape[0]
    width_here = joined_output.shape[1]
    heads_here = width_here // head_size
    blocks = joined_output.reshape(row_count, heads_here, head_size)
    half_size = head_size // 2
    freq_index = jnp.arange(half_size).astype(jnp.float32)
    inverse = jnp.exp(freq_index * (-2.0 / head_size) * math.log(ROPE_BASE))
    angles = positions.astype(jnp.float32)[:, None] * inverse[None, :]
    cosine = jnp.cos(angles)[:, None, :]
    sine_part = jnp.sin(angles)[:, None, :]
    first_half = blocks[:, :, :half_size]
    second_half = blocks[:, :, half_size:]
    turned = jnp.concatenate(
        [
            first_half * cosine - second_half * sine_part,
            second_half * cosine + first_half * sine_part,
        ],
        axis=2,
    )
    head_ids = column_start // head_size + jnp.arange(heads_here)
    is_key = (head_ids % 2 == 0)[None, :, None]
    return jnp.where(is_key, turned, blocks).reshape(row_count, width_here)


def partial_down(block_of_rows, local_index, adapter_down_weight):
    storage_count = adapter_down_weight.shape[0]
    slot_hits = (local_index[:, None] == jnp.arange(storage_count)[None, :]).astype(jnp.float32)
    projected_output = jnp.einsum(
        "he,beg->hbg", block_of_rows, adapter_down_weight, preferred_element_type=jnp.float32
    )
    return jnp.sum(projected_output * slot_hits[:, :, None], axis=1)


def up_products(reduced_state, local_index, adapter_up_weight, key_column_set):
    storage_count = adapter_up_weight.shape[0]
    rank_width = adapter_up_weight.shape[1]
    slot_hits = (local_index[:, None] == jnp.arange(storage_count)[None, :]).astype(jnp.bfloat16)
    key_reduced = slot_hits[:, :, None] * reduced_state[:, None, :rank_width]
    value_reduced = slot_hits[:, :, None] * reduced_state[:, None, rank_width:]
    key_portion = jnp.einsum(
        "imj,mja->ia", key_reduced, adapter_up_weight, preferred_element_type=jnp.float32
    )
    value_portion = jnp.einsum(
        "imj,mja->ia", value_reduced, adapter_up_weight, preferred_element_type=jnp.float32
    )
    return jnp.where(key_column_set[None, :], key_portion, value_portion).astype(jnp.bfloat16)


def blockwise(function, arrays, block_size):
    total_rows = arrays[0].shape[0]
    block_count = total_rows // block_size
    shaped_in = tuple((item.reshape((block_count, block_size) + item.shape[1:]) for item in arrays))
    result = lax.map(function, shaped_in)
    return result.reshape((total_rows,) + result.shape[2:])


def local(
    tokens,
    attention_norm_gain,
    key_value_weight,
    adapter_down_weight,
    adapter_up_weight,
    request_adapter,
    adapter_storage_row,
    cached_token_length,
):
    storage_count = adapter_down_weight.shape[0]
    column_list = adapter_up_weight.shape[2]
    values = tokens.astype(jnp.float32)
    squares = lax.psum(jnp.sum(values * values, axis=1), "tensor")
    scale_row = lax.rsqrt(squares / MODEL_WIDTH + EPSILON)
    normed = (
        values * scale_row[:, None] * attention_norm_gain.astype(jnp.float32)[None, :]
    ).astype(jnp.bfloat16)
    partial_value = jnp.dot(normed, key_value_weight, preferred_element_type=jnp.float32)
    base_product = lax.psum_scatter(partial_value, "tensor", scatter_dimension=1, tiled=True)
    adapter_total = adapter_storage_row.shape[0]
    matches = request_adapter[:, None] == jnp.arange(adapter_total)[None, :]
    stored = jnp.sum(jnp.where(matches, adapter_storage_row[None, :], 0), axis=1)
    column_start = lax.axis_index("tensor") * column_list
    key_column_set = (column_start + jnp.arange(column_list)) // HEAD % 2 == 0
    all_rows, all_stored = (
        lax.all_gather(normed, "wide", axis=0, tiled=True),
        lax.all_gather(stored, "wide", axis=0, tiled=True),
    )
    all_local = all_stored - lax.axis_index("wide") * storage_count
    total_rows = all_rows.shape[0]
    block_size = math.gcd(total_rows, 512)

    def first_section(piece_list):
        return partial_down(piece_list[0], piece_list[1], adapter_down_weight)

    rank_partial = blockwise(first_section, (all_rows, all_local), block_size)
    reduced_state = lax.psum(rank_partial, "tensor").astype(jnp.bfloat16)

    def second_section(piece_list):
        return up_products(piece_list[0], piece_list[1], adapter_up_weight, key_column_set)

    delta_all = blockwise(second_section, (reduced_state, all_local), block_size)
    row_delta = lax.psum_scatter(delta_all, "wide", scatter_dimension=0, tiled=True).astype(
        jnp.float32
    )
    joined_output = base_product + row_delta
    return rotate_keys(joined_output, cached_token_length, column_start, HEAD).astype(jnp.bfloat16)


def solution(mesh):
    return jax.shard_map(
        local,
        mesh=mesh,
        in_specs=(
            P(("parts", "wide"), "tensor"),
            P("tensor"),
            P("tensor", None),
            P(("parts", "wide"), "tensor", None),
            P(("parts", "wide"), None, "tensor"),
            P(("parts", "wide")),
            P("parts"),
            P(("parts", "wide")),
        ),
        out_specs=P(("parts", "wide"), "tensor"),
        check_vma=False,
    )
```

profile of v0, /device:TPU:0, one launch (start us, length us, event | category | flops | bytes accessed | tf_op | source)
XLA Modules:
  0.0 135.9 jit_solution(14912668777077364620)
XLA Ops:
  7.4 0.7 convert_element_type.46
  8.1 1.5 %fusion.25 = f32[256]{0:T(256)S(1)} fusion(bf16[256,2048]{1,0:T(8,128)(2,1)} %param.12), kind=kLoop, calls=%fused_computation.42 | loop fusion | flops 1572608 | bytes 1049600 | tf_op jit(solution)/shard_map/reduce_sum | solution.py:86
  9.6 13.5 %psum.14 = f32[256]{0:T(256)S(1)} all-reduce(f32[256]{0:T(256)S(1)} %fusion.25), channel_id=1, replica_groups=mesh['parts'=2,'wide'=4,'tensor'=4] {'tensor'}, use_global_device_ids=true, to_apply=%region_1.0 | all-reduce | flops 256 | bytes 2048 | tf_op jit(solution)/shard_map/psum | solution.py:86
  23.0 2.5 %fusion.27 = bf16[256,2048]{1,0:T(8,128)(2,1)} fusion(bf16[256,2048]{1,0:T(8,128)(2,1)} %param.12, f32[2048]{0:T(1024)S(1)} %convert_element_type.46, f32[256]{0:T(256)S(1)} %add_rsqrt_fusion), kind=kLoop, calls=%fused_computation.44 | loop fusion | flops 2097152 | bytes 2106368 | tf_op jit(solution)/shard_map/convert_element_type | solution.py:90
  25.6 7.4 %fusion.32 = f32[256,2048]{1,0:T(8,128)} fusion(bf16[256,2048]{1,0:T(8,128)(2,1)} %fusion.27, bf16[2048,2048]{1,0:T(8,128)(2,1)} %param.14), kind=kOutput, calls=%fused_computation.65 | convolution fusion | flops 2147483648 | bytes 11534336 | tf_op jit(solution)/shard_map/dot_general | solution.py:91
  33.1 0.6 copy-done.1
  33.8 5.1 %all-gather = s32[4,1,256]{2,1,0:T(1,128)S(1)} all-gather(s32[1,1,256]{2,1,0:T(1,128)S(1)} %bitcast.73), channel_id=1, replica_groups=mesh['parts'=2,'wide'=4,'tensor'=4] {'wide'}, dimensions={0}, use_global_device_ids=true | all-gather | bytes 5120 | tf_op jit(solution)/shard_map/all_gather | solution.py:100
  38.9 19.6 %all-gather.3.cloned.1.call-done = bf16[1024,2048]{1,0:T(8,128)(2,1)} async-done(((bf16[256,2048]{1,0:T(8,128)(2,1)}), bf16[1024,2048]{1,0:T(8,128)(2,1)}) %all-gather.3.cloned.1.call-update) | async-done | bytes 4194320 | tf_op jit(solution)/shard_map/all_gather | solution.py:99
  58.5 10.6 %while.21 = (s32[]{:T(128)}, f32[2,512,128]{2,1,0:T(8,128)S(1)}, bf16[2,512,2048]{2,1,0:T(8,128)(2,1)}, bf16[8,2048,128]{2,1,0:T(8,128)(2,1)}, s32[2,512]{1,0:T(2,128)S(1)}, /*index=5*/s32[]{:T(128)}) while((s32[]{:T(128)}, f32[2,512,128]{2,1,0:T(8,128)S(1)}, bf16[2,512,2048]{2,1,0:T(8,128)(2,1)}, bf16[8,2048,128]{2,1,0:T(8,128)(2,1)}, ...), condition=%wide.region_6.7_spmd, body=%wide.region_4.6_spmd.sunk | while | flops 2148474880 | bytes 7117389 | solution.py:69
  58.5 5.2 %multiply_reduce_fusion.2 = f32[512,128]{1,0:T(8,128)S(1)} fusion(f32[512,8]{0,1:T(8,128)S(1)} %fusion.51, bf16[8,2048,128]{2,1,0:T(8,128)(2,1)} %get-tuple-element.214, bf16[2,512,2048]{2,1,0:T(8,128)(2,1)} %get-tuple-element.213, s32[]{:T(128)} %get-tuple-element.205), kind=kOutput, calls=%fused_computation.3.clone.1 | convolution fusion | flops 2148466688 | bytes 6570496 | tf_op jit(solution)/shard_map/while/body/eval_jaxpr/he,beg->hbg/dot_general | solution.py:44
  63.8 5.2 %multiply_reduce_fusion.2 = f32[512,128]{1,0:T(8,128)S(1)} fusion(f32[512,8]{0,1:T(8,128)S(1)} %fusion.51, bf16[8,2048,128]{2,1,0:T(8,128)(2,1)} %get-tuple-element.214, bf16[2,512,2048]{2,1,0:T(8,128)(2,1)} %get-tuple-element.213, s32[]{:T(128)} %get-tuple-element.205), kind=kOutput, calls=%fused_computation.3.clone.1 | convolution fusion | flops 2148466688 | bytes 6570496 | tf_op jit(solution)/shard_map/while/body/eval_jaxpr/he,beg->hbg/dot_general | solution.py:44
  69.1 30.5 %all-reduce.1 = bf16[1024,128]{1,0:T(8,128)(2,1)S(1)} all-reduce(f32[1024,128]{1,0:T(8,128)S(1)} %bitcast.70), channel_id=1, replica_groups=mesh['parts'=2,'wide'=4,'tensor'=4] {'tensor'}, use_global_device_ids=true, to_apply=%region_7.8 | all-reduce | flops 131072 | bytes 786432 | tf_op jit(solution)/shard_map/psum | solution.py:110
  99.5 2.4 %while.22 = (s32[]{:T(128)}, bf16[2,512,512]{2,1,0:T(8,128)(2,1)S(1)}, s32[2,512]{1,0:T(2,128)S(1)}, bf16[2,512,128]{2,1,0:T(8,128)(2,1)S(1)}, bf16[8,64,512]{2,1,0:T(8,128)(2,1)S(1)}, /*index=5*/s32[]{:T(128)}, s32[]{:T(128)}) while((s32[]{:T(128)}, bf16[2,512,512]{2,1,0:T(8,128)(2,1)S(1)}, s32[2,512]{1,0:T(2,128)S(1)}, ...), condition=%wide.region_9.10_spmd.clone, body=%wide.region_8.9_spmd.clone.sunk | while | flops 537679872 | bytes 3570781 | solution.py:69
  99.7 0.5 convolution_bitcast_fusion.3
  100.2 0.5 fusion.59
  100.9 0.5 convolution_bitcast_fusion.3
  101.5 0.5 fusion.59
  102.0 1.0 copy-done
  103.1 0.5 multiply_cosine_fusion
  103.7 21.7 %reduce-scatter.5.cloned.1.call-done = bf16[256,512]{1,0:T(8,128)(2,1)} async-done(((bf16[1024,512]{1,0:T(8,128)(2,1)}), bf16[256,512]{1,0:T(8,128)(2,1)}) %reduce-scatter.5.cloned.1.call-update) | async-done | bytes 262160 | tf_op jit(solution)/shard_map/reduce_scatter | solution.py:116
  125.4 1.2 convert_add_fusion
  126.8 0.5 multiply_subtract_fusion
  127.3 0.4 pad_maximum_fusion
  127.7 0.8 fusion.28
  (44 shorter events, 1.0 us)
Async XLA Ops:
  7.4 51.1 %all-gather.3.cloned.1.call-start = ((), (), s32[]{:S(2)}) async-start(), calls=%async_computation.3 | async-start | bytes 5242880 | tf_op jit(solution)/shard_map/all_gather | solution.py:99
  25.6 78.1 %reduce-scatter.3.cloned.1.call-start = ((), (), s32[]{:S(2)}) async-start(), calls=%async_computation.2 | async-start | bytes 2621440 | tf_op jit(solution)/shard_map/reduce_scatter | solution.py:92
  33.0 0.7 copy-start.1
  33.0 0.7 copy-start.3
  33.1 92.4 %reduce-scatter.5.cloned.1.call-start = ((), (), s32[]{:S(2)}) async-start(), calls=%async_computation.4 | async-start | bytes 1310720 | tf_op jit(solution)/shard_map/reduce_scatter | solution.py:116
  58.5 41.0 %copy-start.4 = (bf16[8,64,512]{2,1,0:T(8,128)(2,1)S(1)}, bf16[8,64,512]{2,1,0:T(8,128)(2,1)}, u32[]{:S(2)}) copy-start(bf16[8,64,512]{2,1,0:T(8,128)(2,1)} %param.16) | copy-start | bytes 1572868
  99.5 3.5 %copy-start.2 = (s32[256]{0:T(256)S(1)}, s32[256]{0:T(256)}, u32[]{:S(2)}) copy-start(s32[256]{0:T(256)} %param.19) | copy-start | bytes 3076
  102.0 1.0 copy-start
Sparse Core Ops, SparseCore 0:
  25.7 32.7 all-gather.2
Sparse Core Ops, SparseCore 1:
  33.1 41.7 reduce-scatter.2
  103.1 22.3 reduce-scatter.4
where the time goes:
time: 136 us
  blocking collectives  49 us (36%)
  waiting for transfers between devices  41.4 us (30%)
  matrix products  19.7 us (14%)
  between operations  15 us (11%)
  other arithmetic  8.32 us (6%)
  local copies, waits for them, and re-layouts  2.21 us (2%)
    psum x1, blocking collectives, local(): reduced_state = lax.psum(rank_partial, 'tensor').astype(jnp.bfloat16)  30.5 us
    reduce_scatter x1, waiting for transfers between devices, local(): lax.psum_scatter(delta_all, 'wide', scatter_dimension=0, tiled=True)  21.7 us
    all_gather x1, waiting for transfers between devices, local(): lax.all_gather(normed, 'wide', axis=0, tiled=True)  19.6 us
    psum x1, blocking collectives, local(): squares = lax.psum(jnp.sum(values * values, axis=1), 'tensor')  13.5 us
    dot_general x2, matrix products, partial_down(): jnp.einsum('he,beg->hbg', block_of_rows, adapter_down_weight, preferred_e...  10.4 us
    dot_general x1, matrix products, local(): jnp.dot(normed, key_value_weight, preferred_element_type=jnp.float32)  7.38 us
    all_gather x1, blocking collectives, local(): lax.all_gather(stored, 'wide', axis=0, tiled=True)  5.06 us
  transfers between devices with their start and end apart: 3, of which 2 were waited for; matrix products, arithmetic and copies ran while one was open for 15% of the time, Pallas kernels for 0%

commit v1 on v0

v1 whole, which is shorter than its diff:
```python
import functools
import math

import jax
import jax.numpy as jnp
from jax import lax
from jax.experimental import pallas as pl
from jax.experimental.pallas import tpu as pltpu
from jax.sharding import PartitionSpec as P

MODEL_WIDTH = 8192
HEAD = 128
EPSILON = 1e-05
ROPE_BASE = 500000.0
VMEM_LIMIT = 48 * 1024 * 1024
F32 = jnp.float32
BF16 = jnp.bfloat16


def params():
    return pltpu.CompilerParams(vmem_limit_bytes=VMEM_LIMIT)


def whole():
    return pl.BlockSpec(memory_space=pltpu.VMEM)


def smem():
    return pl.BlockSpec(memory_space=pltpu.SMEM)


def iota(shape, axis):
    return lax.broadcasted_iota(jnp.int32, shape, axis)


def prep_kernel(n_wide, per_dev, cap, cols, table, me_ref, req_ref, tok_ref, gain_ref, *outs):
    xs, ss = outs[:n_wide], outs[n_wide : 2 * n_wide]
    xg_ref, sq_ref = outs[2 * n_wide :]
    rows, depth = tok_ref.shape
    me = me_ref[0]
    req = req_ref[...]
    stored = jnp.zeros_like(req)
    for a in range(table.shape[0]):
        stored = jnp.where(req == a, table[a], stored)
    owner = lax.div(stored, per_dev)
    slot = (stored - owner * per_dev).astype(F32)
    xg = (tok_ref[...].astype(F32) * gain_ref[...].astype(F32)).astype(BF16)
    xg_ref[...] = xg
    pad = -(-n_wide // 16) * 16
    dest = iota((pad, rows), 0) ^ me
    hit = owner == dest
    earlier = (iota((rows, rows), 0) <= iota((rows, rows), 1)).astype(BF16)
    count = jnp.dot(hit.astype(BF16), earlier, preferred_element_type=F32)
    place = jnp.where(hit, count.astype(jnp.int32) - 1, -1)
    for k in [*range(n_wide - 1, 0, -1), 0]:
        pick = iota((cap, rows), 0) == place[k : k + 1]
        sel = pick.astype(BF16)
        ss[k][...] = sel
        xs[k][:, :depth] = jnp.dot(sel, xg, preferred_element_type=F32).astype(BF16)
        slots = jnp.sum(jnp.where(pick, slot, 0.0), axis=1, keepdims=True)
        xs[k][:, depth:] = jnp.broadcast_to(slots, (cap, HEAD)).astype(BF16)
    tok = tok_ref[...]
    gram = lax.dot_general(tok, tok, (((1,), (1,)), ((), ())), preferred_element_type=F32)
    diag = iota((rows, rows), 0) == iota((rows, rows), 1)
    sq = jnp.sum(jnp.where(diag, gram, 0.0), axis=0, keepdims=True)
    width = min(rows, cols)
    terms = []
    for _ in range(3):
        part = sq.astype(BF16).astype(F32)
        sq = sq - part
        terms += [part[:, i : i + width] for i in range(0, rows, width)]
    block = jnp.zeros((16, width), F32)
    for i, term in enumerate(terms):
        block = jnp.where(iota((16, width), 0) == i, term, block)
    if width < cols:
        block = jnp.concatenate([block, jnp.zeros((16, cols - width), F32)], axis=1)
    sq_ref[...] = block.astype(BF16)


def base_kernel(pos_ref, xg_ref, w_ref, sq_ref, out_ref, acc_ref):
    step = pl.program_id(0)
    y = jnp.dot(xg_ref[...], w_ref[...], preferred_element_type=F32)

    @pl.when(step == 0)
    def _():
        acc_ref[...] = y

    @pl.when(step > 0)
    def _():
        acc_ref[...] += y

    @pl.when(step == pl.num_programs(0) - 1)
    def _():
        rows = xg_ref.shape[0]
        out_ref[:rows] = acc_ref[...].astype(out_ref.dtype)
        out_ref[rows:] = sq_ref[...].astype(out_ref.dtype)


def base_block(block, xg, weight, sq, dtype):
    rows, depth = xg.shape
    cols = sq.shape[1]
    chunk = math.gcd(depth, 512)
    return pl.pallas_call(
        base_kernel,
        out_shape=jax.ShapeDtypeStruct((rows + 16, cols), dtype),
        grid_spec=pltpu.PrefetchScalarGridSpec(
            num_scalar_prefetch=1,
            grid=(depth // chunk,),
            in_specs=[
                pl.BlockSpec((rows, chunk), lambda i, p: (0, i)),
                pl.BlockSpec((chunk, cols), lambda i, p: (i, p[0])),
                pl.BlockSpec((16, cols), lambda i, p: (0, 0)),
            ],
            out_specs=pl.BlockSpec((rows + 16, cols), lambda i, p: (0, 0)),
            scratch_shapes=[pltpu.VMEM((rows, cols), F32)],
        ),
        compiler_params=params(),
        cost_estimate=pl.CostEstimate(
            flops=2 * rows * depth * cols, bytes_accessed=2 * depth * cols, transcendentals=0
        ),
        name="base_block",
    )(block, xg, weight, sq)


def down_kernel(count, *refs):
    xs, down_ref, out_ref, acc_ref = refs[:count], refs[count], refs[count + 1], refs[count + 2]
    step = pl.program_id(0)
    depth = down_ref.shape[1]
    pair = jnp.concatenate([down_ref[0], down_ref[1]], axis=1)
    for j in range(count):
        y = jnp.dot(xs[j][:, :depth], pair, preferred_element_type=F32)
        slot = xs[j][:, depth:].astype(F32).astype(jnp.int32)
        z = jnp.where(slot == 2 * step, y[:, :HEAD], 0.0)
        z = jnp.where(slot == 2 * step + 1, y[:, HEAD:], z)

        @pl.when(step == 0)
        def _():
            acc_ref[j] = z

        @pl.when(step > 0)
        def _():
            acc_ref[j] += z

        @pl.when(step == pl.num_programs(0) - 1)
        def _():
            out_ref[j] = acc_ref[j].astype(BF16)


def down_block(xs, down):
    count = len(xs)
    cap, width = xs[0].shape
    per_dev, depth, rank = down.shape
    return pl.pallas_call(
        functools.partial(down_kernel, count),
        out_shape=jax.ShapeDtypeStruct((count, cap, rank), BF16),
        grid=(per_dev // 2,),
        in_specs=[pl.BlockSpec((cap, width), lambda i: (0, 0)) for _ in xs]
        + [pl.BlockSpec((2, depth, rank), lambda i: (i, 0, 0))],
        out_specs=pl.BlockSpec((count, cap, rank), lambda i: (0, 0, 0)),
        scratch_shapes=[pltpu.VMEM((count, cap, rank), F32)],
        compiler_params=params(),
        cost_estimate=pl.CostEstimate(
            flops=2 * count * cap * depth * rank * per_dev,
            bytes_accessed=2 * per_dev * depth * rank,
            transcendentals=0,
        ),
        name="down_block",
    )(*xs, down)


def head_is_key(parity, heads, h):
    if heads % 2 == 0:
        return h % 2 == 0
    return (parity + h) % 2 == 0


def up_kernel(count, n_tensor, parity_ref, *refs):
    slots = refs[:count]
    parts = refs[count : count + n_tensor]
    up_ref = refs[count + n_tensor]
    outs = refs[count + n_tensor + 1 :]
    per_dev, half, cols = up_ref.shape
    heads = cols // HEAD
    up = up_ref[...].reshape(per_dev * half, cols)
    for j in range(count):
        low = parts[0][j].astype(F32)
        for part in parts[1:]:
            low = low + part[j].astype(F32)
        cap, rank = low.shape
        left = iota((cap, rank), 1) < half
        turned = pltpu.roll(low, half, 1)
        slot = slots[j][...].astype(F32).astype(jnp.int32)
        wide = []
        for source in (jnp.where(left, low, turned), jnp.where(left, turned, low)):
            pieces = []
            for g in range(per_dev // 2):
                mine = slot == 2 * g + jnp.where(left, 0, 1)
                pieces.append(jnp.where(mine, source, 0.0).astype(BF16))
            wide.append(jnp.concatenate(pieces, axis=1))
        for h in range(heads):
            key = head_is_key(parity_ref[0], heads, h)
            if isinstance(key, bool):
                lhs = wide[0] if key else wide[1]
            else:
                lhs = jnp.where(key, wide[0].astype(F32), wide[1].astype(F32)).astype(BF16)
            span = slice(h * HEAD, (h + 1) * HEAD)
            outs[j][:, span] = jnp.dot(lhs, up[:, span], preferred_element_type=F32).astype(BF16)


def up_block(parity, slots, parts, up):
    count, cap, _ = parts[0].shape
    cols = up.shape[2]
    return pl.pallas_call(
        functools.partial(up_kernel, count, len(parts)),
        out_shape=[jax.ShapeDtypeStruct((cap, cols), BF16)] * count,
        in_specs=[smem()] + [whole()] * (count + len(parts) + 1),
        out_specs=[whole()] * count,
        compiler_params=params(),
        name="up_block",
    )(parity, *slots, *parts, up)


def final_kernel(n_wide, n_tensor, parity_ref, *refs):
    base = refs[:n_tensor]
    deltas = refs[n_tensor : n_tensor + n_wide]
    sels = refs[n_tensor + n_wide : n_tensor + 2 * n_wide]
    cos_ref, sin_ref, out_ref = refs[n_tensor + 2 * n_wide :]
    rows, cols = out_ref.shape
    width = min(rows, cols)
    tails = [b[rows:].astype(F32) for b in base]
    tail = sum(tails[1:], tails[0])
    pieces = rows // width
    squares = []
    for i in range(pieces):
        total = tail[i : i + 1]
        for p in range(1, 3):
            total = total + tail[p * pieces + i : p * pieces + i + 1]
        squares.append(total[:, :width])
    square = squares[0] if pieces == 1 else jnp.concatenate(squares, axis=1)
    diag = iota((rows, rows), 0) == iota((rows, rows), 1)
    square = jnp.sum(jnp.where(diag, square, 0.0), axis=1, keepdims=True)
    scale = lax.rsqrt(square * (1.0 / MODEL_WIDTH) + EPSILON)
    total = base[0][:rows].astype(F32)
    for b in base[1:]:
        total = total + b[:rows].astype(F32)
    for sel, delta in zip(sels, deltas):
        total = total + lax.dot_general(
            sel[...], delta[...], (((0,), (0,)), ((), ())), preferred_element_type=F32
        )
    total = total * scale
    heads = cols // HEAD
    for h in range(heads):
        span = slice(h * HEAD, (h + 1) * HEAD)
        x = total[:, span]
        key = head_is_key(parity_ref[0], heads, h)
        if key is False:
            out_ref[:, span] = x.astype(BF16)
            continue
        y = x * cos_ref[...] + pltpu.roll(x, HEAD // 2, 1) * sin_ref[...]
        if key is not True:
            y = jnp.where(key, y, x)
        out_ref[:, span] = y.astype(BF16)


def local(
    mesh_shape,
    tokens,
    attention_norm_gain,
    key_value_weight,
    adapter_down_weight,
    adapter_up_weight,
    request_adapter,
    adapter_storage_row,
    cached_token_length,
):
    n_wide, n_tensor = mesh_shape["wide"], mesh_shape["tensor"]
    rows, depth = tokens.shape
    per_dev = adapter_down_weight.shape[0]
    cols = adapter_up_weight.shape[2]
    cap = 104 if n_wide <= 4 else 64
    me = lax.axis_index("wide").astype(jnp.int32).reshape(1)
    spot = lax.axis_index("tensor").astype(jnp.int32)
    parity = (spot * (cols // HEAD) % 2).reshape(1)

    def over(axis, size, array, k):
        return lax.ppermute(array, axis, [(i, i ^ k) for i in range(size)])

    prep = pl.pallas_call(
        functools.partial(prep_kernel, n_wide, per_dev, cap, cols),
        out_shape=[jax.ShapeDtypeStruct((cap, depth + HEAD), BF16)] * n_wide
        + [jax.ShapeDtypeStruct((cap, rows), BF16)] * n_wide
        + [
            jax.ShapeDtypeStruct((rows, depth), BF16),
            jax.ShapeDtypeStruct((16, cols), BF16),
        ],
        in_specs=[smem(), smem(), whole(), whole(), whole()],
        out_specs=[whole()] * (2 * n_wide + 2),
        compiler_params=params(),
        name="prep",
    )(
        adapter_storage_row,
        me,
        request_adapter.reshape(1, rows),
        tokens,
        attention_norm_gain.reshape(1, depth),
    )
    sent, sels = prep[:n_wide], prep[n_wide : 2 * n_wide]
    xg, sq = prep[2 * n_wide :]

    held = [sent[0]] + [None] * (n_wide - 1)
    for k in range(n_wide - 1, 0, -1):
        held[k] = over("wide", n_wide, sent[k], k)

    base = [None] * n_tensor
    for k in range(n_tensor - 1, 0, -1):
        block = base_block((spot ^ k).reshape(1), xg, key_value_weight, sq, BF16)
        base[k] = over("tensor", n_tensor, block, k)
    base[0] = base_block(spot.reshape(1), xg, key_value_weight, sq, F32)

    half_size = HEAD // 2
    freq_index = jnp.arange(half_size).astype(F32)
    inverse = jnp.exp(freq_index * (-2.0 / HEAD) * math.log(ROPE_BASE))
    angles = cached_token_length.astype(F32)[:, None] * inverse[None, :]
    cosine, sine = jnp.cos(angles), jnp.sin(angles)
    cosine = jnp.concatenate([cosine, cosine], axis=1)
    sine = jnp.concatenate([-sine, sine], axis=1)

    deltas = [None] * n_wide
    for group in (range(0, 2), range(2, n_wide)):
        chunk = [held[k] for k in group]
        slots = [x[:, depth:] for x in chunk]
        low = down_block(chunk, adapter_down_weight)
        parts = [low] + [over("tensor", n_tensor, low, k) for k in range(1, n_tensor)]
        ups = up_block(parity, slots, parts, adapter_up_weight)
        for k, delta in zip(group, ups):
            deltas[k] = delta if k == 0 else over("wide", n_wide, delta, k)

    return pl.pallas_call(
        functools.partial(final_kernel, n_wide, n_tensor),
        out_shape=jax.ShapeDtypeStruct((rows, cols), BF16),
        in_specs=[smem()] + [whole()] * (n_tensor + 2 * n_wide + 2),
        out_specs=whole(),
        compiler_params=params(),
        name="finish",
    )(parity, *base, *deltas, *sels, cosine, sine)


def solution(mesh):
    return jax.shard_map(
        functools.partial(local, dict(mesh.shape)),
        mesh=mesh,
        in_specs=(
            P(("parts", "wide"), "tensor"),
            P("tensor"),
            P("tensor", None),
            P(("parts", "wide"), "tensor", None),
            P(("parts", "wide"), None, "tensor"),
            P(("parts", "wide")),
            P("parts"),
            P(("parts", "wide")),
        ),
        out_specs=P(("parts", "wide"), "tensor"),
        check_vma=False,
    )
```

time: 136 us -> 84.9 us (0.62)
  blocking collectives: 49 us -> 0 us
  Pallas kernels: 0 us -> 29.8 us
  starting transfers between devices: 0.09 us -> 22.5 us
  waiting for transfers between devices: 41.4 us -> 20.2 us
  matrix products: 19.7 us -> 0 us
  between operations: 15 us -> 0.21 us
  local copies, waits for them, and re-layouts: 2.21 us -> 10.2 us
  other arithmetic: 8.32 us -> 1.43 us
    psum x2 -> x0, blocking collectives: 43.9 us -> none  [the longest x1 30.5 us: local(): reduced_state = lax.psum(rank_partial, 'tensor').astype(jnp.bfloat16)]
    pallas_call x0 -> x10, Pallas kernels: none -> 29.8 us  [the longest x4 15.5 us: base_block(): pl.pallas_call(base_kernel, out_shape=jax.ShapeDtypeStruct((rows + 16, co...]
    ppermute x0 -> x15, starting transfers between devices: none -> 22.5 us  [over(): return lax.ppermute(array, axis, [(i, i ^ k) for i in range(size)])]
    reduce_scatter x2 -> x0, waiting for transfers between devices: 21.8 us -> none  [the longest x1 21.7 us: local(): lax.psum_scatter(delta_all, 'wide', scatter_dimension=0, tiled=True)]
    ppermute x0 -> x15, waiting for transfers between devices: none -> 20.2 us  [over(): return lax.ppermute(array, axis, [(i, i ^ k) for i in range(size)])]
    dot_general x7 -> x0, matrix products: 19.7 us -> none  [the longest x2 10.4 us: partial_down(): jnp.einsum('he,beg->hbg', block_of_rows, adapter_down_weight, preferred_e...]
    all_gather x1 -> x0, waiting for transfers between devices: 19.6 us -> none  [local(): lax.all_gather(normed, 'wide', axis=0, tiled=True)]
    unnamed x10 -> x36, local copies, waits for them, and re-layouts: 1.57 us -> 9.45 us
  transfers between devices with their start and end apart: 3 -> 15, of which waited for: 2 -> 5; matrix products, arithmetic and copies ran while one was open for 15% -> 2% of each run, Pallas kernels for 0% -> 30%
where the time goes in v1:
time: 84.9 us; the launch traced here: 84.3 us
  Pallas kernels  29.8 us (35%)
  starting transfers between devices  22.5 us (27%)
  waiting for transfers between devices  20.2 us (24%)
  local copies, waits for them, and re-layouts  10.2 us (12%)
  other arithmetic  1.43 us (2%)
    ppermute x15, starting transfers between devices, over(): return lax.ppermute(array, axis, [(i, i ^ k) for i in range(size)])  22.5 us
    ppermute x15, waiting for transfers between devices, over(): return lax.ppermute(array, axis, [(i, i ^ k) for i in range(size)])  20.2 us
    pallas_call x4, Pallas kernels, base_block(): pl.pallas_call(base_kernel, out_shape=jax.ShapeDtypeStruct((rows + 16, co...  15.5 us
    unnamed x36, local copies, waits for them, and re-layouts  9.45 us
    pallas_call x2, Pallas kernels, down_block(): pl.pallas_call(functools.partial(down_kernel, count), out_shape=jax.Shape...  6.83 us
    pallas_call x2, Pallas kernels, up_block(): pl.pallas_call(functools.partial(up_kernel, count, len(parts)), out_shape...  2.63 us
    pallas_call x1, Pallas kernels, local(): pl.pallas_call(functools.partial(prep_kernel, n_wide, per_dev, cap, cols)...  2.49 us
    pallas_call x1, Pallas kernels, local(): pl.pallas_call(functools.partial(final_kernel, n_wide, n_tensor), out_sha...  2.39 us
  transfers between devices with their start and end apart: 15, of which 5 were waited for; matrix products, arithmetic and copies ran while one was open for 2% of the time, Pallas kernels for 30%

profile of v1, /device:TPU:0, one launch (start us, length us, event | category | flops | bytes accessed | tf_op | source)
XLA Modules:
  0.0 84.3 jit_solution(3014456866261280226)
XLA Ops:
  3.3 2.5 %prep.1 = (bf16[104,2176]{1,0:T(8,128)(2,1)S(1)}, bf16[104,2176]{1,0:T(8,128)(2,1)S(1)}, bf16[104,2176]{1,0:T(8,128)(2,1)}, bf16[104,2176]{1,0:T(8,128)(2,1)}, b...) custom-call(s32[32]{0:T(128)S(1)} %copy-done.13, ...), custom_call_target="tpu_custom_call" | custom-call | tf_op jit(solution)/shard_map/prep/pallas_call | solution.py:288
  8.2 2.9 %collective-permute-start.8 = (bf16[104,2176]{1,0:T(8,128)(2,1)}, bf16[104,2176]{1,0:T(8,128)(2,1)S(1)}, u32[]{:S(2)}, u32[]{:S(2)}) collective-permute-start(bf16[104,2176]{1,0:T(8,128)(2,1)} %get-tuple-element.25), channel_id=1, source_target_pairs={{0,8},{4,12},{8,0},{12,4},{1,9},{5,13},{9,1},{13,5},{2,10},{6,14},... | collective-permute-start | bytes 1357832 | tf_op jit(solution)/shard_map/ppermute | solution.py:286
  11.3 4.0 %base_block.7 = bf16[272,512]{1,0:T(8,128)(2,1)} custom-call(s32[1]{0:T(128)} %bitcast.6.pos_ref, bf16[256,2048]{1,0:T(8,128)(2,1)S(1)} %get-tuple-element.19.xg_ref, bf16[2048,2048]{1,0:T(8,128)(2,1)} %w_ref.7, bf16[16,512]{1,0:T(8,128)(2,1)S(1)} %get-tuple-element.20.sq_ref), custom_call_target="tpu_custom_call" | custom-call | flops 536870912 | bytes 2097152 | tf_op jit(solution)/shard_map/base_block/pallas_call | solution.py:103
  15.3 4.1 %collective-permute-start.2 = (bf16[272,512]{1,0:T(8,128)(2,1)}, bf16[272,512]{1,0:T(8,128)(2,1)}, u32[]{:S(2)}, u32[]{:S(2)}) collective-permute-start(bf16[272,512]{1,0:T(8,128)(2,1)} %base_block.7), channel_id=1, source_target_pairs={{0,3},{1,2},{2,1},{3,0},{4,7},{5,6},{6,5},{7,4},{8,11},{9,10},{10,... | collective-permute-start | bytes 835592 | tf_op jit(solution)/shard_map/ppermute | solution.py:286
  19.4 3.2 %collective-permute-done.8.refs_0_ = bf16[104,2176]{1,0:T(8,128)(2,1)S(1)} collective-permute-done((bf16[104,2176]{1,0:T(8,128)(2,1)}, bf16[104,2176]{1,0:T(8,128)(2,1)S(1)}, u32[]{:S(2)}, u32[]{:S(2)}) %collective-permute-start.8) | collective-permute-done | bytes 452640 | tf_op jit(solution)/shard_map/ppermute | solution.py:286
  22.6 8.2 %collective-permute-done.9.refs_1_ = bf16[104,2176]{1,0:T(8,128)(2,1)S(1)} collective-permute-done((bf16[104,2176]{1,0:T(8,128)(2,1)}, bf16[104,2176]{1,0:T(8,128)(2,1)S(1)}, u32[]{:S(2)}, u32[]{:S(2)}) %collective-permute-start.9) | collective-permute-done | bytes 452640 | tf_op jit(solution)/shard_map/ppermute | solution.py:286
  30.8 2.2 %copy-done = bf16[8,2048,128]{2,1,0:T(8,128)(2,1)S(1)} copy-done((bf16[8,2048,128]{2,1,0:T(8,128)(2,1)S(1)}, bf16[8,2048,128]{2,1,0:T(8,128)(2,1)}, u32[]{:S(2)}) %copy-start) | copy-done | bytes 4194328
  33.0 3.4 %down_block.3.refs_2_ = bf16[2,104,128]{2,1,0:T(8,128)(2,1)S(1)} custom-call(bf16[104,2176]{1,0:T(8,128)(2,1)S(1)} %collective-permute-done.8.refs_0_, bf16[104,2176]{1,0:T(8,128)(2,1)S(1)} %collective-permute-done.9.refs_1_, bf16[8,2048,128]{2,1,0:T(8,128)(2,1)S(1)} %copy-done), custom_call_target="tpu_custom_call" | custom-call | flops 872415232 | bytes 4194304 | tf_op jit(solution)/shard_map/down_block/pallas_call | solution.py:153
  36.5 1.6 %collective-permute-start.10 = (bf16[2,104,128]{2,1,0:T(8,128)(2,1)S(1)}, bf16[2,104,128]{2,1,0:T(8,128)(2,1)}, u32[]{:S(2)}, u32[]{:S(2)}) collective-permute-start(bf16[2,104,128]{2,1,0:T(8,128)(2,1)S(1)} %down_block.3.refs_2_), channel_id=1, source_target_pairs={{0,1},{1,0},{2,3},{3,2},{4,5},{5,4},{6,7},{7,6},{8,9},{9,8},{10,11... | collective-permute-start | bytes 159752 | tf_op jit(solution)/shard_map/ppermute | solution.py:286
  38.1 2.6 %collective-permute-start.11 = (bf16[2,104,128]{2,1,0:T(8,128)(2,1)S(1)}, bf16[2,104,128]{2,1,0:T(8,128)(2,1)}, u32[]{:S(2)}, u32[]{:S(2)}) collective-permute-start(bf16[2,104,128]{2,1,0:T(8,128)(2,1)S(1)} %down_block.3.refs_2_), channel_id=1, source_target_pairs={{0,2},{1,3},{2,0},{3,1},{4,6},{5,7},{6,4},{7,5},{8,10},{9,11},{10,... | collective-permute-start | bytes 159752 | tf_op jit(solution)/shard_map/ppermute | solution.py:286
  40.9 2.2 %copy-done.1 = bf16[8,2048,128]{2,1,0:T(8,128)(2,1)S(1)} copy-done((bf16[8,2048,128]{2,1,0:T(8,128)(2,1)S(1)}, bf16[8,2048,128]{2,1,0:T(8,128)(2,1)}, u32[]{:S(2)}) %copy-start.1) | copy-done | bytes 4194328
  43.1 3.4 %down_block.2.refs_2_ = bf16[2,104,128]{2,1,0:T(8,128)(2,1)S(1)} custom-call(bf16[104,2176]{1,0:T(8,128)(2,1)S(1)} %get-tuple-element.21.refs_0_, bf16[104,2176]{1,0:T(8,128)(2,1)S(1)} %collective-permute-done.3.refs_1_, bf16[8,2048,128]{2,1,0:T(8,128)(2,1)S(1)} %copy-done.1), custom_call_target="tpu_custom_call" | custom-call | flops 872415232 | bytes 4194304 | tf_op jit(solution)/shard_map/down_block/pallas_call | solution.py:153
  47.3 4.0 %base_block.6 = bf16[272,512]{1,0:T(8,128)(2,1)} custom-call(s32[1]{0:T(128)} %bitcast.5.pos_ref, bf16[256,2048]{1,0:T(8,128)(2,1)S(1)} %get-tuple-element.19.xg_ref, bf16[2048,2048]{1,0:T(8,128)(2,1)} %w_ref.7, bf16[16,512]{1,0:T(8,128)(2,1)S(1)} %get-tuple-element.20.sq_ref), custom_call_target="tpu_custom_call" | custom-call | flops 536870912 | bytes 2097152 | tf_op jit(solution)/shard_map/base_block/pallas_call | solution.py:103
  51.3 4.1 %base_block.5 = bf16[272,512]{1,0:T(8,128)(2,1)} custom-call(s32[1]{0:T(128)} %bitcast.4.pos_ref, bf16[256,2048]{1,0:T(8,128)(2,1)S(1)} %get-tuple-element.19.xg_ref, bf16[2048,2048]{1,0:T(8,128)(2,1)} %w_ref.7, bf16[16,512]{1,0:T(8,128)(2,1)S(1)} %get-tuple-element.20.sq_ref), custom_call_target="tpu_custom_call" | custom-call | flops 536870912 | bytes 2097152 | tf_op jit(solution)/shard_map/base_block/pallas_call | solution.py:103
  55.3 3.5 %collective-permute-start.1 = (bf16[272,512]{1,0:T(8,128)(2,1)}, bf16[272,512]{1,0:T(8,128)(2,1)}, u32[]{:S(2)}, u32[]{:S(2)}) collective-permute-start(bf16[272,512]{1,0:T(8,128)(2,1)} %base_block.6), channel_id=1, source_target_pairs={{0,2},{1,3},{2,0},{3,1},{4,6},{5,7},{6,4},{7,5},{8,10},{9,11},{10,... | collective-permute-start | bytes 835592 | tf_op jit(solution)/shard_map/ppermute | solution.py:286
  59.6 3.6 %collective-permute-start.6 = (bf16[2,104,128]{2,1,0:T(8,128)(2,1)S(1)}, bf16[2,104,128]{2,1,0:T(8,128)(2,1)}, u32[]{:S(2)}, u32[]{:S(2)}) collective-permute-start(bf16[2,104,128]{2,1,0:T(8,128)(2,1)S(1)} %down_block.2.refs_2_), channel_id=1, source_target_pairs={{0,3},{1,2},{2,1},{3,0},{4,7},{5,6},{6,5},{7,4},{8,11},{9,10},{10,... | collective-permute-start | bytes 159752 | tf_op jit(solution)/shard_map/ppermute | solution.py:286
  64.6 3.4 %base_block.4.refs_0_ = f32[272,512]{1,0:T(8,128)S(1)} custom-call(s32[1]{0:T(128)} %bitcast.1.pos_ref, bf16[256,2048]{1,0:T(8,128)(2,1)S(1)} %get-tuple-element.19.xg_ref, bf16[2048,2048]{1,0:T(8,128)(2,1)} %w_ref.7, bf16[16,512]{1,0:T(8,128)(2,1)S(1)} %get-tuple-element.20.sq_ref), custom_call_target="tpu_custom_call" | custom-call | flops 536870912 | bytes 2097152 | tf_op jit(solution)/shard_map/base_block/pallas_call | solution.py:103
  68.1 1.3 %up_block.3 = (bf16[104,512]{1,0:T(8,128)(2,1)S(1)}, bf16[104,512]{1,0:T(8,128)(2,1)S(1)}) custom-call(s32[1]{0:T(128)} %bitcast.parity_ref, bf16[104,128]{1,0:T(8,128)(2,1)S(1)} %slice.17.refs_0_, bf16[104,128]{1,0:T(8,128)(2,1)S(1)} %slice.18.refs_1_, bf16[2,104,128]{2,1,0:T(8,128)(2,1)S(1)} %down_block.3.refs_2_, ...), custom_call_target="tpu_custom_call" | custom-call | tf_op jit(solution)/shard_map/up_block/pallas_call | solution.py:213
  69.4 5.7 %collective-permute-done.5.refs_4_ = bf16[2,104,128]{2,1,0:T(8,128)(2,1)} collective-permute-done((bf16[2,104,128]{2,1,0:T(8,128)(2,1)S(1)}, bf16[2,104,128]{2,1,0:T(8,128)(2,1)}, u32[]{:S(2)}, u32[]{:S(2)}) %collective-permute-start.5) | collective-permute-done | bytes 53280 | tf_op jit(solution)/shard_map/ppermute | solution.py:286
  75.1 1.5 %collective-permute-start.13 = (bf16[104,512]{1,0:T(8,128)(2,1)S(1)}, bf16[104,512]{1,0:T(8,128)(2,1)S(1)}, u32[]{:S(2)}, u32[]{:S(2)}) collective-permute-start(bf16[104,512]{1,0:T(8,128)(2,1)S(1)} %get-tuple-element.27), channel_id=1, source_target_pairs={{0,8},{4,12},{8,0},{12,4},{1,9},{5,13},{9,1},{13,5},{2,10},{6,14},... | collective-permute-start | bytes 319496 | tf_op jit(solution)/shard_map/ppermute | solution.py:286
  76.6 1.3 %up_block.2 = (bf16[104,512]{1,0:T(8,128)(2,1)S(1)}, bf16[104,512]{1,0:T(8,128)(2,1)S(1)}) custom-call(s32[1]{0:T(128)} %bitcast.parity_ref, bf16[104,128]{1,0:T(8,128)(2,1)S(1)} %slice.12.refs_0_, bf16[104,128]{1,0:T(8,128)(2,1)S(1)} %slice.16.refs_1_, bf16[2,104,128]{2,1,0:T(8,128)(2,1)S(1)} %down_block.2.refs_2_, ...), custom_call_target="tpu_custom_call" | custom-call | tf_op jit(solution)/shard_map/up_block/pallas_call | solution.py:213
  78.8 1.4 %collective-permute-done.13.refs_6_ = bf16[104,512]{1,0:T(8,128)(2,1)S(1)} collective-permute-done((bf16[104,512]{1,0:T(8,128)(2,1)S(1)}, bf16[104,512]{1,0:T(8,128)(2,1)S(1)}, u32[]{:S(2)}, u32[]{:S(2)}) %collective-permute-start.13) | collective-permute-done | bytes 106528 | tf_op jit(solution)/shard_map/ppermute | solution.py:286
  80.3 1.6 %collective-permute-done.14.refs_7_ = bf16[104,512]{1,0:T(8,128)(2,1)S(1)} collective-permute-done((bf16[104,512]{1,0:T(8,128)(2,1)S(1)}, bf16[104,512]{1,0:T(8,128)(2,1)S(1)}, u32[]{:S(2)}, u32[]{:S(2)}) %collective-permute-start.14) | collective-permute-done | bytes 106528 | tf_op jit(solution)/shard_map/ppermute | solution.py:286
  81.9 2.4 %finish.1 = bf16[256,512]{1,0:T(8,128)(2,1)} custom-call(s32[1]{0:T(128)} %bitcast.parity_ref, f32[272,512]{1,0:T(8,128)S(1)} %base_block.4.refs_0_, bf16[272,512]{1,0:T(8,128)(2,1)} %collective-permute-done.refs_1_, bf16[272,512]{1,0:T(8,128)(2,1)} %collective-permute-done.1.refs_2_, bf16[272,512]{1,0:T(8,128)(2,1)} %collective-permute-done.2.refs_3_, ...), custom_call_target="tpu_custom_call" | custom-call | tf_op jit(solution)/shard_map/finish/pallas_call | solution.py:338
  (61 shorter events, 9.9 us)
Async XLA Ops:
  8.2 14.4 %collective-permute-start.8 = (bf16[104,2176]{1,0:T(8,128)(2,1)}, bf16[104,2176]{1,0:T(8,128)(2,1)S(1)}, u32[]{:S(2)}, u32[]{:S(2)}) collective-permute-start(bf16[104,2176]{1,0:T(8,128)(2,1)} %get-tuple-element.25), channel_id=1, source_target_pairs={{0,8},{4,12},{8,0},{12,4},{1,9},{5,13},{9,1},{13,5},{2,10},{6,14},... | collective-permute-start | bytes 1357832 | tf_op jit(solution)/shard_map/ppermute | solution.py:286
  11.2 19.7 %collective-permute-start.9 = (bf16[104,2176]{1,0:T(8,128)(2,1)}, bf16[104,2176]{1,0:T(8,128)(2,1)S(1)}, u32[]{:S(2)}, u32[]{:S(2)}) collective-permute-start(bf16[104,2176]{1,0:T(8,128)(2,1)} %get-tuple-element.26), channel_id=1, source_target_pairs={{0,12},{4,8},{8,4},{12,0},{1,13},{5,9},{9,5},{13,1},{2,14},{6,10},... | collective-permute-start | bytes 1357832 | tf_op jit(solution)/shard_map/ppermute | solution.py:286
  11.2 29.7 %collective-permute-start.3 = (bf16[104,2176]{1,0:T(8,128)(2,1)S(1)}, bf16[104,2176]{1,0:T(8,128)(2,1)S(1)}, u32[]{:S(2)}, u32[]{:S(2)}) collective-permute-start(bf16[104,2176]{1,0:T(8,128)(2,1)S(1)} %get-tuple-element.22), channel_id=1, source_target_pairs={{0,4},{4,0},{8,12},{12,8},{1,5},{5,1},{9,13},{13,9},{2,6},{6,2},{1... | collective-permute-start | bytes 1357832 | tf_op jit(solution)/shard_map/ppermute | solution.py:286
  15.3 62.6 %collective-permute-start.2 = (bf16[272,512]{1,0:T(8,128)(2,1)}, bf16[272,512]{1,0:T(8,128)(2,1)}, u32[]{:S(2)}, u32[]{:S(2)}) collective-permute-start(bf16[272,512]{1,0:T(8,128)(2,1)} %base_block.7), channel_id=1, source_target_pairs={{0,3},{1,2},{2,1},{3,0},{4,7},{5,6},{6,5},{7,4},{8,11},{9,10},{10,... | collective-permute-start | bytes 835592 | tf_op jit(solution)/shard_map/ppermute | solution.py:286
  36.4 14.8 %copy-start.17 = (s32[256]{0:T(256)S(1)}, s32[256]{0:T(256)}, u32[]{:S(2)}) copy-start(s32[256]{0:T(256)} %param.15) | copy-start | bytes 3076
  36.5 18.9 %collective-permute-start.10 = (bf16[2,104,128]{2,1,0:T(8,128)(2,1)S(1)}, bf16[2,104,128]{2,1,0:T(8,128)(2,1)}, u32[]{:S(2)}, u32[]{:S(2)}) collective-permute-start(bf16[2,104,128]{2,1,0:T(8,128)(2,1)S(1)} %down_block.3.refs_2_), channel_id=1, source_target_pairs={{0,1},{1,0},{2,3},{3,2},{4,5},{5,4},{6,7},{7,6},{8,9},{9,8},{10,11... | collective-permute-start | bytes 159752 | tf_op jit(solution)/shard_map/ppermute | solution.py:286
  38.1 20.8 %collective-permute-start.11 = (bf16[2,104,128]{2,1,0:T(8,128)(2,1)S(1)}, bf16[2,104,128]{2,1,0:T(8,128)(2,1)}, u32[]{:S(2)}, u32[]{:S(2)}) collective-permute-start(bf16[2,104,128]{2,1,0:T(8,128)(2,1)S(1)} %down_block.3.refs_2_), channel_id=1, source_target_pairs={{0,2},{1,3},{2,0},{3,1},{4,6},{5,7},{6,4},{7,5},{8,10},{9,11},{10,... | collective-permute-start | bytes 159752 | tf_op jit(solution)/shard_map/ppermute | solution.py:286
  40.7 18.2 %collective-permute-start.12 = (bf16[2,104,128]{2,1,0:T(8,128)(2,1)S(1)}, bf16[2,104,128]{2,1,0:T(8,128)(2,1)}, u32[]{:S(2)}, u32[]{:S(2)}) collective-permute-start(bf16[2,104,128]{2,1,0:T(8,128)(2,1)S(1)} %down_block.3.refs_2_), channel_id=1, source_target_pairs={{0,3},{1,2},{2,1},{3,0},{4,7},{5,6},{6,5},{7,4},{8,11},{9,10},{10,... | collective-permute-start | bytes 159752 | tf_op jit(solution)/shard_map/ppermute | solution.py:286
  46.5 13.1 %collective-permute-start.4 = (bf16[2,104,128]{2,1,0:T(8,128)(2,1)S(1)}, bf16[2,104,128]{2,1,0:T(8,128)(2,1)}, u32[]{:S(2)}, u32[]{:S(2)}) collective-permute-start(bf16[2,104,128]{2,1,0:T(8,128)(2,1)S(1)} %down_block.2.refs_2_), channel_id=1, source_target_pairs={{0,1},{1,0},{2,3},{3,2},{4,5},{5,4},{6,7},{7,6},{8,9},{9,8},{10,11... | collective-permute-start | bytes 159752 | tf_op jit(solution)/shard_map/ppermute | solution.py:286
  51.3 16.8 %copy-start.2 = (bf16[8,64,512]{2,1,0:T(8,128)(2,1)S(1)}, bf16[8,64,512]{2,1,0:T(8,128)(2,1)}, u32[]{:S(2)}) copy-start(bf16[8,64,512]{2,1,0:T(8,128)(2,1)} %refs_6_.3) | copy-start | bytes 1572868
  55.3 23.5 %collective-permute-start.1 = (bf16[272,512]{1,0:T(8,128)(2,1)}, bf16[272,512]{1,0:T(8,128)(2,1)}, u32[]{:S(2)}, u32[]{:S(2)}) collective-permute-start(bf16[272,512]{1,0:T(8,128)(2,1)} %base_block.6), channel_id=1, source_target_pairs={{0,2},{1,3},{2,0},{3,1},{4,6},{5,7},{6,4},{7,5},{8,10},{9,11},{10,... | collective-permute-start | bytes 835592 | tf_op jit(solution)/shard_map/ppermute | solution.py:286
  58.8 20.0 %collective-permute-start = (bf16[272,512]{1,0:T(8,128)(2,1)}, bf16[272,512]{1,0:T(8,128)(2,1)}, u32[]{:S(2)}, u32[]{:S(2)}) collective-permute-start(bf16[272,512]{1,0:T(8,128)(2,1)} %base_block.5), channel_id=1, source_target_pairs={{0,1},{1,0},{2,3},{3,2},{4,5},{5,4},{6,7},{7,6},{8,9},{9,8},{10,11... | collective-permute-start | bytes 835592 | tf_op jit(solution)/shard_map/ppermute | solution.py:286
  58.9 16.3 %collective-permute-start.5 = (bf16[2,104,128]{2,1,0:T(8,128)(2,1)S(1)}, bf16[2,104,128]{2,1,0:T(8,128)(2,1)}, u32[]{:S(2)}, u32[]{:S(2)}) collective-permute-start(bf16[2,104,128]{2,1,0:T(8,128)(2,1)S(1)} %down_block.2.refs_2_), channel_id=1, source_target_pairs={{0,2},{1,3},{2,0},{3,1},{4,6},{5,7},{6,4},{7,5},{8,10},{9,11},{10,... | collective-permute-start | bytes 159752 | tf_op jit(solution)/shard_map/ppermute | solution.py:286
  59.6 17.0 %collective-permute-start.6 = (bf16[2,104,128]{2,1,0:T(8,128)(2,1)S(1)}, bf16[2,104,128]{2,1,0:T(8,128)(2,1)}, u32[]{:S(2)}, u32[]{:S(2)}) collective-permute-start(bf16[2,104,128]{2,1,0:T(8,128)(2,1)S(1)} %down_block.2.refs_2_), channel_id=1, source_target_pairs={{0,3},{1,2},{2,1},{3,0},{4,7},{5,6},{6,5},{7,4},{8,11},{9,10},{10,... | collective-permute-start | bytes 159752 | tf_op jit(solution)/shard_map/ppermute | solution.py:286
  64.5 14.2 %copy-start.14 = (f32[256,64]{1,0:T(8,128)S(1)}, f32[256,64]{1,0:T(8,128)}, u32[]{:S(2)}) copy-start(f32[256,64]{1,0:T(8,128)} %get-tuple-element.33) | copy-start | bytes 196612
  64.5 17.3 %copy-start.5 = (bf16[104,256]{1,0:T(8,128)(2,1)S(1)}, bf16[104,256]{1,0:T(8,128)(2,1)}, u32[]{:S(2)}) copy-start(bf16[104,256]{1,0:T(8,128)(2,1)} %copy-done.4) | copy-start | bytes 159748
  64.5 17.3 %copy-start.7 = (bf16[104,256]{1,0:T(8,128)(2,1)S(1)}, bf16[104,256]{1,0:T(8,128)(2,1)}, u32[]{:S(2)}) copy-start(bf16[104,256]{1,0:T(8,128)(2,1)} %copy-done.6) | copy-start | bytes 159748
  64.5 17.3 %copy-start.9 = (bf16[104,256]{1,0:T(8,128)(2,1)S(1)}, bf16[104,256]{1,0:T(8,128)(2,1)}, u32[]{:S(2)}) copy-start(bf16[104,256]{1,0:T(8,128)(2,1)} %copy-done.8) | copy-start | bytes 159748
  64.5 17.3 %copy-start.11 = (bf16[104,256]{1,0:T(8,128)(2,1)S(1)}, bf16[104,256]{1,0:T(8,128)(2,1)}, u32[]{:S(2)}) copy-start(bf16[104,256]{1,0:T(8,128)(2,1)} %copy-done.10) | copy-start | bytes 159748
  64.6 14.1 %copy-start.15 = (f32[256,64]{1,0:T(8,128)S(1)}, f32[256,64]{1,0:T(8,128)}, u32[]{:S(2)}) copy-start(f32[256,64]{1,0:T(8,128)} %get-tuple-element.34) | copy-start | bytes 196612
  64.6 14.1 %copy-start.16 = (f32[256,64]{1,0:T(8,128)S(1)}, f32[256,64]{1,0:T(8,128)}, u32[]{:S(2)}) copy-start(f32[256,64]{1,0:T(8,128)} %get-tuple-element.35) | copy-start | bytes 196612
  75.1 5.1 %collective-permute-start.13 = (bf16[104,512]{1,0:T(8,128)(2,1)S(1)}, bf16[104,512]{1,0:T(8,128)(2,1)S(1)}, u32[]{:S(2)}, u32[]{:S(2)}) collective-permute-start(bf16[104,512]{1,0:T(8,128)(2,1)S(1)} %get-tuple-element.27), channel_id=1, source_target_pairs={{0,8},{4,12},{8,0},{12,4},{1,9},{5,13},{9,1},{13,5},{2,10},{6,14},... | collective-permute-start | bytes 319496 | tf_op jit(solution)/shard_map/ppermute | solution.py:286
  76.6 5.2 %collective-permute-start.14 = (bf16[104,512]{1,0:T(8,128)(2,1)S(1)}, bf16[104,512]{1,0:T(8,128)(2,1)S(1)}, u32[]{:S(2)}, u32[]{:S(2)}) collective-permute-start(bf16[104,512]{1,0:T(8,128)(2,1)S(1)} %get-tuple-element.28), channel_id=1, source_target_pairs={{0,12},{4,8},{8,4},{12,0},{1,13},{5,9},{9,5},{13,1},{2,14},{6,10},... | collective-permute-start | bytes 319496 | tf_op jit(solution)/shard_map/ppermute | solution.py:286
  77.9 3.9 %collective-permute-start.7 = (bf16[104,512]{1,0:T(8,128)(2,1)S(1)}, bf16[104,512]{1,0:T(8,128)(2,1)S(1)}, u32[]{:S(2)}, u32[]{:S(2)}) collective-permute-start(bf16[104,512]{1,0:T(8,128)(2,1)S(1)} %get-tuple-element.24), channel_id=1, source_target_pairs={{0,4},{4,0},{8,12},{12,8},{1,5},{5,1},{9,13},{13,9},{2,6},{6,2},{1... | collective-permute-start | bytes 319496 | tf_op jit(solution)/shard_map/ppermute | solution.py:286
  (9 other events, 9.4 us)
